TPU v7x, 32 devices: a whole 2x2x4 slice. The times are simulated.
32 devices in a mesh: rep: 1, row: 8 (over y, x, core), col: 4 (over z).
Axes of the slice: x: 2, y: 2, z: 4, core: 2. Of those that a mesh axis runs over, the one named last changes fastest.
Arguments:
- tokens: bfloat16 [4096, 1024], P(('rep', 'row', 'col')), may hold values from -6 to 6
- out_grad: bfloat16 [4096, 1024], P(('rep', 'row', 'col')), may hold values from -6 to 6
- expert_ids: int32 [4096, 2], P(('rep', 'row', 'col')), may hold values from 0 to 31, all different within a row; in each aligned block of 128 rows (0 to 127, 128 to 255, ...) at most 12 rows name the same one
- gates: float32 [4096, 2], P(('rep', 'row', 'col')), may hold values from 0.25 to 1
- up_weight: bfloat16 [32, 1024, 4096], P(('row', 'col'), None, 'rep'), may hold values from -0.1875 to 0.1875
- down_weight: bfloat16 [32, 4096, 1024], P(('row', 'col'), 'rep'), may hold values from -0.09375 to 0.09375
Outputs:
- input_grad: bfloat16 [4096, 1024], P(('rep', 'row', 'col'))
- down_grad: bfloat16 [32, 4096, 1024], P(('row', 'col'), 'rep')
Inputs may be any that keep to these rules, and one draw needn't show every extreme that they name: `expert_ids`: in the 128 rows of one device no expert is named more than 12 times; in every draw some expert is named exactly 12 times in such a block.
All inputs are finite; a program needn't handle non-finite values.
Results may differ from a plain program's by a relative error of at most 0.013.
Values may be sent and summed in bfloat16 or wider, within the bound.
No kernel may reach another device: no remote copies, remote signals or barrier semaphores. Data moves between devices by JAX's collectives and lax.ppermute only.
A program may use at most 64 MiB of HBM per device.

v0:
```python
import functools

import jax
import jax.numpy as jnp
from jax import lax
from jax.experimental import pallas as pl
from jax.experimental.pallas import tpu as pltpu
from jax.sharding import PartitionSpec as P

VMEM_LIMIT = 48 * 1024 * 1024
PAIR = 2
TILE = 1024
AHEAD = 2
NOWHERE = -(1 << 20)


def f32_dot(lhs, rhs, contract=((1,), (0,))):
    return lax.dot_general(lhs, rhs, (contract, ((), ())), preferred_element_type=jnp.float32)


def params():
    return pltpu.CompilerParams(vmem_limit_bytes=VMEM_LIMIT)


def row_places(ids, experts, capacity):
    tok_rows = ids.shape[1]
    names = lax.broadcasted_iota(jnp.int32, (experts, tok_rows), 0)
    chosen = [names == ids[k : k + 1, :] for k in range(ids.shape[0])]
    member = functools.reduce(jnp.logical_or, chosen).astype(jnp.bfloat16)
    before = (
        lax.broadcasted_iota(jnp.int32, (tok_rows, tok_rows), 0)
        < lax.broadcasted_iota(jnp.int32, (tok_rows, tok_rows), 1)
    ).astype(jnp.bfloat16)
    rank = f32_dot(member, before).astype(jnp.int32)
    place = names * (PAIR * capacity) + rank
    return [jnp.sum(jnp.where(pick, place, 0), axis=0, keepdims=True) for pick in chosen]


def hits_at(rows, places):
    at = lax.broadcasted_iota(jnp.int32, (rows, places[0].shape[1]), 0)
    return [at == place for place in places]


def either(hits):
    return functools.reduce(jnp.logical_or, hits).astype(jnp.bfloat16)


def started(pairs, sems):
    copies = [pltpu.make_async_copy(*pair, sems.at[i]) for i, pair in enumerate(pairs)]
    for copy in copies:
        copy.start()
    return copies


def dispatch_kernel(capacity, *refs):
    sources, (out_ref, ids_ref, gates_ref, both_ref, sems) = refs[:4], refs[4:]
    tok_rows = both_ref.shape[0] // 2
    targets = ids_ref, gates_ref, both_ref.at[pl.ds(0, tok_rows)], both_ref.at[pl.ds(tok_rows, tok_rows)]
    ids_copy, gates_copy, tokens_copy, grad_copy = started(zip(sources, targets), sems)
    rows = out_ref.shape[0]
    ids_copy.wait()
    places = row_places(ids_ref[...], rows // (PAIR * capacity), capacity)
    token_hits = hits_at(rows, places)
    grad_hits = hits_at(rows, [place + capacity for place in places])
    gates_copy.wait()
    scales = [jnp.where(hit, 1.0, 0.0) for hit in token_hits]
    scales += [jnp.where(hit, gates_ref[k : k + 1, :], 0.0) for k, hit in enumerate(grad_hits)]
    scale = jnp.sum(sum(scales), axis=1, keepdims=True)
    gather = jnp.concatenate([either(token_hits), either(grad_hits)], axis=1)
    tokens_copy.wait()
    grad_copy.wait()
    out_ref[...] = (scale * f32_dot(gather, both_ref[...])).astype(jnp.bfloat16)


def paired_rows(number, capacity):
    owner = jnp.floor((number.astype(jnp.float32) + 0.5) * (1.0 / capacity)).astype(jnp.int32)
    return number + owner * ((PAIR - 1) * capacity)


def group_size(peers, capacity):
    size = 1
    while peers % (2 * size) == 0 and size * PAIR * capacity < 192:
        size *= 2
    return size


def take_apart(landed_ref, capacity, rows_ref, grads_ref):
    size = group_size(landed_ref.shape[0] // (PAIR * capacity), capacity)
    slots, rows = size * capacity, size * PAIR * capacity
    at = lax.broadcasted_iota(jnp.int32, (slots, rows), 1)
    source = paired_rows(lax.broadcasted_iota(jnp.int32, (slots, 1), 0), capacity)
    mover = jnp.concatenate([(at == source + j * capacity).astype(jnp.bfloat16) for j in range(PAIR)], axis=0)
    for i in range(rows_ref.shape[0] // slots):
        taken = f32_dot(mover, landed_ref[i * rows : (i + 1) * rows, :]).astype(jnp.bfloat16)
        rows_ref[i * slots : (i + 1) * slots, :] = taken[:slots]
        grads_ref[i * slots : (i + 1) * slots, :] = taken[slots:]


def fold_rows(plain_ref, capacity, folded_ref, out_ref, sems):
    size = group_size(plain_ref.shape[0] // capacity, capacity)
    slots, rows = size * capacity, size * PAIR * capacity
    width = folded_ref.shape[1]
    at = lax.broadcasted_iota(jnp.int32, (rows, slots), 0)
    target = paired_rows(lax.broadcasted_iota(jnp.int32, (1, slots), 1), capacity)
    mover = jnp.concatenate([(at == target + j * capacity).astype(jnp.bfloat16) for j in range(PAIR)], axis=1)
    copies = []
    for i in range(plain_ref.shape[0] // slots):
        plain = plain_ref[i * slots : (i + 1) * slots, :].astype(jnp.bfloat16)
        halves = jnp.concatenate([plain[:, j * width : (j + 1) * width] for j in range(PAIR)], axis=0)
        part = slice(i * rows, (i + 1) * rows)
        folded_ref[part, :] = f32_dot(mover, halves).astype(jnp.bfloat16)
        copies.append(pltpu.make_async_copy(folded_ref.at[part], out_ref.at[part], sems.at[i]))
        copies[-1].start()
    return copies


def unit_tiles(units):
    size = min(units, TILE)
    return [(start, size) for start in range(0, units, size)]


def expert_kernel(capacity, landed_ref, up_ref, down_ref, hidden_out, grads_out, back_out, *scratch):
    up, down, rows, grads, hidden, masked, total, back, weight_sems, hidden_sems, grads_sem, back_sems = scratch
    tiles = unit_tiles(up.shape[1])

    def weight_copies(i):
        at = pl.ds(*tiles[i])
        return [
            pltpu.make_async_copy(up_ref.at[:, at], up.at[:, at], weight_sems.at[0, i]),
            pltpu.make_async_copy(down_ref.at[at], down.at[at], weight_sems.at[1, i]),
        ]

    def start_weights(i):
        if i < len(tiles):
            arriving[i] = weight_copies(i)
            for copy in arriving[i]:
                copy.start()

    def add_row_grad(i):
        start, size = tiles[i]
        part = f32_dot(masked[i % 2, :, :size], up[:, start : start + size], ((1,), (1,)))
        total[...] = part if i == 0 else total[...] + part

    arriving, leaving = {}, []
    for i in range(AHEAD):
        start_weights(i)
    take_apart(landed_ref, capacity, rows, grads)
    leaving.append(pltpu.make_async_copy(grads, grads_out, grads_sem.at[0]))
    leaving[-1].start()
    for i, (start, size) in enumerate(tiles):
        here = slice(start, start + size)
        start_weights(i + AHEAD)
        for copy in arriving[i]:
            copy.wait()
        preact = f32_dot(rows[...], up[:, here])
        hidden_grad = f32_dot(grads[...], down[here, :], ((1,), (1,)))
        if i:
            add_row_grad(i - 1)
        hidden[:, here] = jnp.maximum(preact, 0.0).astype(jnp.bfloat16)
        masked[i % 2, :, :size] = jnp.where(preact > 0, hidden_grad, 0.0).astype(jnp.bfloat16)
        leaving.append(pltpu.make_async_copy(hidden.at[:, here], hidden_out.at[:, here], hidden_sems.at[i]))
        leaving[-1].start()
    add_row_grad(len(tiles) - 1)
    for copy in leaving + fold_rows(total, capacity, back, back_out, back_sems):
        copy.wait()


def down_grad_kernel(grads_ref, hidden_ref, out_ref):
    out_ref[...] = f32_dot(hidden_ref[...], grads_ref[...], ((0,), (0,))).astype(jnp.bfloat16)


def pick_map_kernel(capacity, ids_ref, after_ref, out_ref):
    tok_rows, rows = ids_ref.shape[1], out_ref.shape[1]
    places = row_places(ids_ref[...], rows // (PAIR * capacity), capacity)
    for j in range(PAIR):
        chosen = either(hits_at(rows, [place + j * capacity for place in places]))
        out_ref[j * tok_rows : (j + 1) * tok_rows, :] = chosen.T


def pick_kernel(map_ref, returned_ref, out_ref):
    tok_rows, width = out_ref.shape[0], returned_ref.shape[1]
    picked = f32_dot(map_ref[...], returned_ref[...]).astype(jnp.bfloat16)
    for j in range(PAIR):
        out_ref[:, j * width : (j + 1) * width] = picked[j * tok_rows : (j + 1) * tok_rows]


def exchange(rows):
    axes = ("row", "col")
    peers = lax.axis_size(axes)
    cut = rows.reshape(peers, rows.shape[0] // peers, rows.shape[1])
    return lax.all_to_all(cut, axes, split_axis=0, concat_axis=0, tiled=True).reshape(rows.shape)


def in_hbm(array):
    return pltpu.with_memory_space_constraint(array, pltpu.HBM)


def held(rows, columns, kind=jnp.bfloat16):
    return pltpu.VMEM((rows, columns), kind)


def shards(tokens, out_grad, expert_ids, gates, up_weight, down_weight):
    tok_rows, features = tokens.shape
    top_count = expert_ids.shape[1]
    units = up_weight.shape[2]
    peers = lax.axis_size(("row", "col"))
    capacity = 3 * tok_rows * top_count // (2 * peers)
    slots, rows, width = peers * capacity, peers * PAIR * capacity, features // PAIR
    tile = min(units, TILE // 2)
    steps = units // tile
    bf16, f32 = jnp.bfloat16, jnp.float32
    shape = jax.ShapeDtypeStruct
    dma = pltpu.SemaphoreType.DMA
    flops = 2 * slots * features * units
    weight_bytes = 2 * features * units

    def cost(matmuls, weights):
        return pl.CostEstimate(flops=matmuls * flops, bytes_accessed=weights * weight_bytes, transcendentals=0)

    ids = expert_ids.T
    hbm = pl.BlockSpec(memory_space=pltpu.HBM)
    vmem = pl.BlockSpec(memory_space=pltpu.VMEM)
    anywhere = pl.BlockSpec(memory_space=pl.ANY)
    tiles = unit_tiles(units)

    sent = pl.pallas_call(
        functools.partial(dispatch_kernel, capacity),
        out_shape=shape((rows, features), bf16),
        in_specs=[hbm, hbm, hbm, hbm],
        scratch_shapes=[
            held(top_count, tok_rows, jnp.int32),
            held(top_count, tok_rows, f32),
            held(2 * tok_rows, features),
            dma((4,)),
        ],
        compiler_params=params(),
        name="dispatch",
    )(*[in_hbm(array) for array in (ids, gates.T, tokens, out_grad)])
    landed = exchange(sent)

    hidden, grads, back = pl.pallas_call(
        functools.partial(expert_kernel, capacity),
        out_shape=(
            pltpu.HBM((slots, units), bf16),
            pltpu.HBM((slots, features), bf16),
            pltpu.HBM((rows, width), bf16),
        ),
        in_specs=[vmem, hbm, hbm],
        out_specs=(hbm, hbm, hbm),
        scratch_shapes=[
            held(features, units),
            held(units, features),
            held(slots, features),
            held(slots, features),
            held(slots, units),
            pltpu.VMEM((2, slots, tiles[0][1]), bf16),
            held(slots, features, f32),
            held(rows, width),
            dma((2, len(tiles))),
            dma((len(tiles),)),
            dma((1,)),
            dma((peers // group_size(peers, capacity),)),
        ],
        compiler_params=params(),
        cost_estimate=cost(3, 2),
        name="expert",
    )(landed, in_hbm(up_weight[0]), in_hbm(down_weight[0]))
    returned = exchange(back)

    down_grad = pl.pallas_call(
        down_grad_kernel,
        out_shape=shape((1, units, features), bf16),
        grid=(steps,),
        in_specs=[pl.BlockSpec((slots, features), lambda i: (0, 0)), pl.BlockSpec((slots, tile), lambda i: (0, i))],
        out_specs=pl.BlockSpec((None, tile, features), lambda i: (0, i, 0)),
        compiler_params=params(),
        cost_estimate=cost(1, 1),
        name="down_grad",
    )(in_hbm(grads), in_hbm(hidden))

    pick_map = pl.pallas_call(
        functools.partial(pick_map_kernel, capacity),
        out_shape=shape((PAIR * tok_rows, rows), bf16),
        in_specs=[vmem, anywhere],
        compiler_params=params(),
        name="pick_map",
    )(ids, in_hbm(grads))
    input_grad = pl.pallas_call(
        pick_kernel,
        out_shape=shape((tok_rows, features), bf16),
        compiler_params=params(),
        name="pick",
    )(pick_map, returned)
    return input_grad, down_grad


def pooled_shards(tokens, out_grad, expert_ids, gates, up_weight, down_weight):
    tok_rows = tokens.shape[0]
    top_count = expert_ids.shape[1]
    features = tokens.shape[1]
    groups = lax.axis_size("row")
    col_count = lax.axis_size("col")
    experts = groups * col_count
    capacity = 3 * tok_rows * top_count // (2 * experts)
    flat_ids = expert_ids.reshape(-1)
    onehot = (flat_ids[:, None] == jnp.arange(experts, dtype=jnp.int32)[None, :]).astype(jnp.int32)
    earlier = jnp.cumsum(onehot, axis=0) - onehot
    slot_index = jnp.sum(earlier * onehot, axis=1)
    target = flat_ids * capacity + slot_index
    placer = (jnp.arange(experts * capacity, dtype=jnp.int32)[:, None] == target[None, :]).astype(
        jnp.bfloat16
    )
    token_rows = jnp.repeat(tokens, top_count, axis=0)
    weighted = (
        gates.reshape(-1)[:, None] * jnp.repeat(out_grad, top_count, axis=0).astype(jnp.float32)
    ).astype(jnp.bfloat16)
    send_inputs = jnp.dot(placer, token_rows, preferred_element_type=jnp.float32).astype(
        jnp.bfloat16
    )
    send_grads = jnp.dot(placer, weighted, preferred_element_type=jnp.float32).astype(jnp.bfloat16)
    landed_inputs, landed_grads = (
        lax.all_to_all(
            send_inputs.reshape(experts, capacity, features),
            ("row", "col"),
            split_axis=0,
            concat_axis=0,
            tiled=True,
        ),
        lax.all_to_all(
            send_grads.reshape(experts, capacity, features),
            ("row", "col"),
            split_axis=0,
            concat_axis=0,
            tiled=True,
        ),
    )
    pooled_inputs, pooled_grads = (
        lax.all_gather(landed_inputs, "rep", axis=0, tiled=True),
        lax.all_gather(landed_grads, "rep", axis=0, tiled=True),
    )
    slot_rows = pooled_inputs.shape[0] * capacity
    input_rows = pooled_inputs.reshape(slot_rows, features)
    grad_rows = pooled_grads.reshape(slot_rows, features)
    up_block = up_weight[0]
    down_block = down_weight[0]
    preact = jnp.dot(input_rows, up_block, preferred_element_type=jnp.float32)
    hidden = jnp.maximum(preact, 0.0).astype(jnp.bfloat16)
    hidden_grad = lax.dot_general(
        grad_rows, down_block, (((1,), (1,)), ((), ())), preferred_element_type=jnp.float32
    )
    preact_grad = jnp.where(preact > 0, hidden_grad, 0.0).astype(jnp.bfloat16)
    weight_grad = lax.dot_general(
        hidden, grad_rows, (((0,), (0,)), ((), ())), preferred_element_type=jnp.float32
    )
    down_grad = weight_grad.astype(jnp.bfloat16)[None]
    summed_rows = lax.psum_scatter(
        lax.dot_general(
            preact_grad, up_block, (((1,), (1,)), ((), ())), preferred_element_type=jnp.float32
        ).astype(jnp.bfloat16),
        "rep",
        scatter_dimension=0,
        tiled=True,
    )
    returned = lax.all_to_all(
        summed_rows.reshape(experts, capacity, features),
        ("row", "col"),
        split_axis=0,
        concat_axis=0,
        tiled=True,
    )
    returned = returned.reshape(experts * capacity, features)
    picked = lax.dot_general(
        placer, returned, (((0,), (0,)), ((), ())), preferred_element_type=jnp.float32
    )
    input_grad = jnp.sum(picked.reshape(tok_rows, top_count, features), axis=1).astype(jnp.bfloat16)
    return (input_grad, down_grad)


def solution(mesh):
    by_token = P(("rep", "row", "col"), None)
    by_expert = (P(("row", "col"), None, "rep"), P(("row", "col"), "rep", None))
    return jax.shard_map(
        shards if mesh.shape["rep"] == 1 else pooled_shards,
        mesh=mesh,
        in_specs=(by_token,) * 4 + by_expert,
        out_specs=(by_token, by_expert[1]),
        check_vma=False,
    )
```

profile of v0, /device:TPU:1, one launch (start us, length us, event | category | flops | bytes accessed | tf_op | source)
XLA Modules:
  0.0 86.8 jit_solution(10756076224330456461)
XLA Ops:
  0.6 1.9 %dispatch.1 = bf16[768,1024]{1,0:T(8,128)(2,1)S(1)} custom-call(s32[2,128]{1,0:T(2,128)} %bitcast.11, f32[2,128]{1,0:T(2,128)} %bitcast.14, bf16[128,1024]{1,0:T(8,128)(2,1)} %refs_2_.1, bf16[128,1024]{1,0:T(8,128)(2,1)} %refs_3_.1), custom_call_target="tpu_custom_call" | custom-call | tf_op jit(solution)/shard_map/dispatch/pallas_call | solution.py:226
  2.5 44.7 %all_to_all.10 = bf16[32,24,1024]{2,1,0:T(8,128)(2,1)S(1)} all-to-all(bf16[32,24,1024]{2,1,0:T(8,128)(2,1)S(1)} %bitcast.8), channel_id=1, replica_groups=mesh['rep'=1,'row'=8,'col'=4] {'row','col'}, dimensions={0} | all-to-all | bytes 3145728 | tf_op jit(solution)/shard_map/all_to_all | solution.py:191
  47.2 0.0 copy-start
  47.2 14.5 %expert.1 = (bf16[384,4096]{1,0:T(8,128)(2,1)}, bf16[384,1024]{1,0:T(8,128)(2,1)}, bf16[768,512]{1,0:T(8,128)(2,1)}) custom-call(bf16[768,1024]{1,0:T(8,128)(2,1)S(1)} %bitcast.10, bf16[1024,4096]{1,0:T(8,128)(2,1)} %bitcast.15, bf16[4096,1024]{1,0:T(8,128)(2,1)} %bitcast.16), custom_call_target="tpu_custom_call" | custom-call | flops 9663676416 | bytes 16777216 | tf_op jit(solution)/shard_map/expert/pallas_call | solution.py:241
  61.7 3.2 %all-to-all-start.1 = ((bf16[32,24,512]{2,1,0:T(8,128)(2,1)}), bf16[32,24,512]{2,1,0:T(8,128)(2,1)S(1)}, u32[]{:S(2)}, u32[]{:S(2)}) async-start(bf16[32,24,512]{2,1,0:T(8,128)(2,1)} %bitcast.13), calls=%async_computation.1 | async-start | bytes 1572864 | tf_op jit(solution)/shard_map/all_to_all | solution.py:191
  64.9 0.0 copy-done
  64.9 0.3 pick_map.1.map_ref
  65.2 10.1 %down_grad.1 = bf16[1,4096,1024]{2,1,0:T(8,128)(2,1)} custom-call(bf16[384,1024]{1,0:T(8,128)(2,1)} %get-tuple-element.5.after_ref.grads_ref, bf16[384,4096]{1,0:T(8,128)(2,1)} %get-tuple-element.7.hidden_ref), custom_call_target="tpu_custom_call" | custom-call | flops 3221225472 | bytes 8388608 | tf_op jit(solution)/shard_map/down_grad/pallas_call | solution.py:270
  75.3 10.4 %all-to-all-done.1 = bf16[32,24,512]{2,1,0:T(8,128)(2,1)S(1)} async-done(((bf16[32,24,512]{2,1,0:T(8,128)(2,1)}), bf16[32,24,512]{2,1,0:T(8,128)(2,1)S(1)}, u32[]{:S(2)}, u32[]{:S(2)}) %all-to-all-start.1) | async-done | bytes 786464 | tf_op jit(solution)/shard_map/all_to_all | solution.py:191
  85.7 1.1 %pick.1 = bf16[128,1024]{1,0:T(8,128)(2,1)} custom-call(bf16[256,768]{1,0:T(8,128)(2,1)S(1)} %pick_map.1.map_ref, bf16[768,512]{1,0:T(8,128)(2,1)S(1)} %bitcast.9), custom_call_target="tpu_custom_call" | custom-call | tf_op jit(solution)/shard_map/pick/pallas_call | solution.py:288
Async XLA Ops:
  47.2 17.7 %copy-start = (s32[128,2]{0,1:T(2,128)S(1)}, s32[128,2]{0,1:T(2,128)}, u32[]{:S(2)}) copy-start(s32[128,2]{0,1:T(2,128)} %param.8) | copy-start | bytes 3076
  61.7 24.0 %all-to-all-start.1 = ((bf16[32,24,512]{2,1,0:T(8,128)(2,1)}), bf16[32,24,512]{2,1,0:T(8,128)(2,1)S(1)}, u32[]{:S(2)}, u32[]{:S(2)}) async-start(bf16[32,24,512]{2,1,0:T(8,128)(2,1)} %bitcast.13), calls=%async_computation.1 | async-start | bytes 1572864 | tf_op jit(solution)/shard_map/all_to_all | solution.py:191
where the time goes:
time: 87.2 us; the launch traced here: 86.8 us
  blocking collectives  44.7 us (51%)
  Pallas kernels  27.9 us (32%)
  waiting for transfers between devices  10.4 us (12%)
  starting transfers between devices  3.17 us (4%)
    all_to_all x1, blocking collectives, exchange(): lax.all_to_all(cut, axes, split_axis=0, concat_axis=0, tiled=True)  44.7 us
    pallas_call x1, Pallas kernels, shards(): pl.pallas_call(functools.partial(expert_kernel, capacity), out_shape=(plt...  14.5 us
    all_to_all x1, waiting for transfers between devices, exchange(): lax.all_to_all(cut, axes, split_axis=0, concat_axis=0, tiled=True)  10.4 us
    pallas_call x1, Pallas kernels, shards(): pl.pallas_call(down_grad_kernel, out_shape=shape((1, units, features), bf...  10.1 us
    all_to_all x1, starting transfers between devices, exchange(): lax.all_to_all(cut, axes, split_axis=0, concat_axis=0, tiled=True)  3.17 us
    pallas_call x1, Pallas kernels, shards(): pl.pallas_call(functools.partial(dispatch_kernel, capacity), out_shape=sh...  1.89 us
  transfers between devices with their start and end apart: 1, of which 1 were waited for; matrix products, arithmetic and copies ran while one was open for 0% of the time, Pallas kernels for 12%

commit v1 on v0

--- a/solution.py
+++ b/solution.py
@@ -136,11 +136,6 @@
             for copy in arriving[i]:
                 copy.start()
 
-    def add_row_grad(i):
-        start, size = tiles[i]
-        part = f32_dot(masked[i % 2, :, :size], up[:, start : start + size], ((1,), (1,)))
-        total[...] = part if i == 0 else total[...] + part
-
     arriving, leaving = {}, []
     for i in range(AHEAD):
         start_weights(i)
@@ -154,13 +149,11 @@
             copy.wait()
         preact = f32_dot(rows[...], up[:, here])
         hidden_grad = f32_dot(grads[...], down[here, :], ((1,), (1,)))
-        if i:
-            add_row_grad(i - 1)
         hidden[:, here] = jnp.maximum(preact, 0.0).astype(jnp.bfloat16)
-        masked[i % 2, :, :size] = jnp.where(preact > 0, hidden_grad, 0.0).astype(jnp.bfloat16)
+        masked[:, here] = jnp.where(preact > 0, hidden_grad, 0.0).astype(jnp.bfloat16)
         leaving.append(pltpu.make_async_copy(hidden.at[:, here], hidden_out.at[:, here], hidden_sems.at[i]))
         leaving[-1].start()
-    add_row_grad(len(tiles) - 1)
+    total[...] = f32_dot(masked[...], up[...], ((1,), (1,)))
     for copy in leaving + fold_rows(total, capacity, back, back_out, back_sems):
         copy.wait()
 
@@ -253,7 +246,7 @@
             held(slots, features),
             held(slots, features),
             held(slots, units),
-            pltpu.VMEM((2, slots, tiles[0][1]), bf16),
+            held(slots, units),
             held(slots, features, f32),
             held(rows, width),
             dma((2, len(tiles))),

time: 87.2 us -> 87.2 us (level)
  no operation moved by 1% of the time
where the time goes in v1:
time: 87.2 us; the launch traced here: 86.7 us
  blocking collectives  44.7 us (51%)
  Pallas kernels  27.8 us (32%)
  waiting for transfers between devices  10.4 us (12%)
  starting transfers between devices  3.17 us (4%)
    all_to_all x1, blocking collectives, exchange(): lax.all_to_all(cut, axes, split_axis=0, concat_axis=0, tiled=True)  44.7 us
    pallas_call x1, Pallas kernels, shards(): pl.pallas_call(functools.partial(expert_kernel, capacity), out_shape=(plt...  14.4 us
    all_to_all x1, waiting for transfers between devices, exchange(): lax.all_to_all(cut, axes, split_axis=0, concat_axis=0, tiled=True)  10.4 us
    pallas_call x1, Pallas kernels, shards(): pl.pallas_call(down_grad_kernel, out_shape=shape((1, units, features), bf...  10.1 us
    all_to_all x1, starting transfers between devices, exchange(): lax.all_to_all(cut, axes, split_axis=0, concat_axis=0, tiled=True)  3.17 us
    pallas_call x1, Pallas kernels, shards(): pl.pallas_call(functools.partial(dispatch_kernel, capacity), out_shape=sh...  1.89 us
  transfers between devices with their start and end apart: 1, of which 1 were waited for; matrix products, arithmetic and copies ran while one was open for 0% of the time, Pallas kernels for 12%

profile of v1, /device:TPU:1, one launch (start us, length us, event | category | flops | bytes accessed | tf_op | source)
XLA Modules:
  0.0 86.7 jit_solution(8759628142593387124)
XLA Ops:
  0.6 1.9 %dispatch.1 = bf16[768,1024]{1,0:T(8,128)(2,1)S(1)} custom-call(s32[2,128]{1,0:T(2,128)} %bitcast.11, f32[2,128]{1,0:T(2,128)} %bitcast.14, bf16[128,1024]{1,0:T(8,128)(2,1)} %refs_2_.1, bf16[128,1024]{1,0:T(8,128)(2,1)} %refs_3_.1), custom_call_target="tpu_custom_call" | custom-call | tf_op jit(solution)/shard_map/dispatch/pallas_call | solution.py:219
  2.5 44.7 %all_to_all.10 = bf16[32,24,1024]{2,1,0:T(8,128)(2,1)S(1)} all-to-all(bf16[32,24,1024]{2,1,0:T(8,128)(2,1)S(1)} %bitcast.8), channel_id=1, replica_groups=mesh['rep'=1,'row'=8,'col'=4] {'row','col'}, dimensions={0} | all-to-all | bytes 3145728 | tf_op jit(solution)/shard_map/all_to_all | solution.py:184
  47.2 0.0 copy-start
  47.2 14.4 %expert.1 = (bf16[384,4096]{1,0:T(8,128)(2,1)}, bf16[384,1024]{1,0:T(8,128)(2,1)}, bf16[768,512]{1,0:T(8,128)(2,1)}) custom-call(bf16[768,1024]{1,0:T(8,128)(2,1)S(1)} %bitcast.10, bf16[1024,4096]{1,0:T(8,128)(2,1)} %bitcast.15, bf16[4096,1024]{1,0:T(8,128)(2,1)} %bitcast.16), custom_call_target="tpu_custom_call" | custom-call | flops 9663676416 | bytes 16777216 | tf_op jit(solution)/shard_map/expert/pallas_call | solution.py:234
  61.7 3.2 %all-to-all-start.1 = ((bf16[32,24,512]{2,1,0:T(8,128)(2,1)}), bf16[32,24,512]{2,1,0:T(8,128)(2,1)S(1)}, u32[]{:S(2)}, u32[]{:S(2)}) async-start(bf16[32,24,512]{2,1,0:T(8,128)(2,1)} %bitcast.13), calls=%async_computation.1 | async-start | bytes 1572864 | tf_op jit(solution)/shard_map/all_to_all | solution.py:184
  64.8 0.0 copy-done
  64.8 0.3 pick_map.1.map_ref
  65.2 10.1 %down_grad.1 = bf16[1,4096,1024]{2,1,0:T(8,128)(2,1)} custom-call(bf16[384,1024]{1,0:T(8,128)(2,1)} %get-tuple-element.5.after_ref.grads_ref, bf16[384,4096]{1,0:T(8,128)(2,1)} %get-tuple-element.7.hidden_ref), custom_call_target="tpu_custom_call" | custom-call | flops 3221225472 | bytes 8388608 | tf_op jit(solution)/shard_map/down_grad/pallas_call | solution.py:263
  75.3 10.4 %all-to-all-done.1 = bf16[32,24,512]{2,1,0:T(8,128)(2,1)S(1)} async-done(((bf16[32,24,512]{2,1,0:T(8,128)(2,1)}), bf16[32,24,512]{2,1,0:T(8,128)(2,1)S(1)}, u32[]{:S(2)}, u32[]{:S(2)}) %all-to-all-start.1) | async-done | bytes 786464 | tf_op jit(solution)/shard_map/all_to_all | solution.py:184
  85.7 1.1 %pick.1 = bf16[128,1024]{1,0:T(8,128)(2,1)} custom-call(bf16[256,768]{1,0:T(8,128)(2,1)S(1)} %pick_map.1.map_ref, bf16[768,512]{1,0:T(8,128)(2,1)S(1)} %bitcast.9), custom_call_target="tpu_custom_call" | custom-call | tf_op jit(solution)/shard_map/pick/pallas_call | solution.py:281
Async XLA Ops:
  47.2 17.6 %copy-start = (s32[128,2]{0,1:T(2,128)S(1)}, s32[128,2]{0,1:T(2,128)}, u32[]{:S(2)}) copy-start(s32[128,2]{0,1:T(2,128)} %param.8) | copy-start | bytes 3076
  61.7 24.0 %all-to-all-start.1 = ((bf16[32,24,512]{2,1,0:T(8,128)(2,1)}), bf16[32,24,512]{2,1,0:T(8,128)(2,1)S(1)}, u32[]{:S(2)}, u32[]{:S(2)}) async-start(bf16[32,24,512]{2,1,0:T(8,128)(2,1)} %bitcast.13), calls=%async_computation.1 | async-start | bytes 1572864 | tf_op jit(solution)/shard_map/all_to_all | solution.py:184

commit v2 on v0

--- a/solution.py
+++ b/solution.py
@@ -7,7 +7,7 @@
 from jax.experimental.pallas import tpu as pltpu
 from jax.sharding import PartitionSpec as P
 
-VMEM_LIMIT = 48 * 1024 * 1024
+VMEM_LIMIT = 44 * 1024 * 1024
 PAIR = 2
 TILE = 1024
 AHEAD = 2
@@ -53,10 +53,13 @@
 
 
 def dispatch_kernel(capacity, *refs):
-    sources, (out_ref, ids_ref, gates_ref, both_ref, sems) = refs[:4], refs[4:]
+    sources, (up_ref, down_ref, out_ref, up_out, down_out, ids_ref, gates_ref, both_ref, sems) = refs[:4], refs[4:]
     tok_rows = both_ref.shape[0] // 2
     targets = ids_ref, gates_ref, both_ref.at[pl.ds(0, tok_rows)], both_ref.at[pl.ds(tok_rows, tok_rows)]
     ids_copy, gates_copy, tokens_copy, grad_copy = started(zip(sources, targets), sems)
+    first = pl.ds(0, down_out.shape[0])
+    weights = (up_ref.at[:, first], up_out), (down_ref.at[first], down_out)
+    weight_copies = started(weights, sems.at[pl.ds(4, 2)])
     rows = out_ref.shape[0]
     ids_copy.wait()
     places = row_places(ids_ref[...], rows // (PAIR * capacity), capacity)
@@ -70,6 +73,8 @@
     tokens_copy.wait()
     grad_copy.wait()
     out_ref[...] = (scale * f32_dot(gather, both_ref[...])).astype(jnp.bfloat16)
+    for copy in weight_copies:
+        copy.wait()
 
 
 def paired_rows(number, capacity):
@@ -119,7 +124,9 @@
     return [(start, size) for start in range(0, units, size)]
 
 
-def expert_kernel(capacity, landed_ref, up_ref, down_ref, hidden_out, grads_out, back_out, *scratch):
+def expert_kernel(
+    capacity, landed_ref, first_up, first_down, up_ref, down_ref, hidden_out, grads_out, back_out, *scratch
+):
     up, down, rows, grads, hidden, masked, total, back, weight_sems, hidden_sems, grads_sem, back_sems = scratch
     tiles = unit_tiles(up.shape[1])
 
@@ -138,11 +145,12 @@
 
     def add_row_grad(i):
         start, size = tiles[i]
-        part = f32_dot(masked[i % 2, :, :size], up[:, start : start + size], ((1,), (1,)))
+        weights = up[:, start : start + size] if i else first_up[...]
+        part = f32_dot(masked[i % 2, :, :size], weights, ((1,), (1,)))
         total[...] = part if i == 0 else total[...] + part
 
     arriving, leaving = {}, []
-    for i in range(AHEAD):
+    for i in range(1, AHEAD):
         start_weights(i)
     take_apart(landed_ref, capacity, rows, grads)
     leaving.append(pltpu.make_async_copy(grads, grads_out, grads_sem.at[0]))
@@ -150,10 +158,10 @@
     for i, (start, size) in enumerate(tiles):
         here = slice(start, start + size)
         start_weights(i + AHEAD)
-        for copy in arriving[i]:
+        for copy in arriving.get(i, ()):
             copy.wait()
-        preact = f32_dot(rows[...], up[:, here])
-        hidden_grad = f32_dot(grads[...], down[here, :], ((1,), (1,)))
+        preact = f32_dot(rows[...], up[:, here] if i else first_up[...])
+        hidden_grad = f32_dot(grads[...], down[here, :] if i else first_down[...], ((1,), (1,)))
         if i:
             add_row_grad(i - 1)
         hidden[:, here] = jnp.maximum(preact, 0.0).astype(jnp.bfloat16)
@@ -193,6 +201,10 @@
 
 def in_hbm(array):
     return pltpu.with_memory_space_constraint(array, pltpu.HBM)
+
+
+def in_vmem(array):
+    return pltpu.with_memory_space_constraint(array, pltpu.VMEM)
 
 
 def held(rows, columns, kind=jnp.bfloat16):
@@ -223,19 +235,25 @@
     anywhere = pl.BlockSpec(memory_space=pl.ANY)
     tiles = unit_tiles(units)
 
-    sent = pl.pallas_call(
+    size = tiles[0][1]
+    weights = in_hbm(up_weight[0]), in_hbm(down_weight[0])
+    sent, first_up, first_down = pl.pallas_call(
         functools.partial(dispatch_kernel, capacity),
-        out_shape=shape((rows, features), bf16),
-        in_specs=[hbm, hbm, hbm, hbm],
+        out_shape=(
+            shape((rows, features), bf16),
+            pltpu.VMEM((features, size), bf16),
+            pltpu.VMEM((size, features), bf16),
+        ),
+        in_specs=[hbm, hbm, hbm, hbm, hbm, hbm],
         scratch_shapes=[
             held(top_count, tok_rows, jnp.int32),
             held(top_count, tok_rows, f32),
             held(2 * tok_rows, features),
-            dma((4,)),
+            dma((6,)),
         ],
         compiler_params=params(),
         name="dispatch",
-    )(*[in_hbm(array) for array in (ids, gates.T, tokens, out_grad)])
+    )(*[in_hbm(array) for array in (ids, gates.T, tokens, out_grad)], *weights)
     landed = exchange(sent)
 
     hidden, grads, back = pl.pallas_call(
@@ -245,7 +263,7 @@
             pltpu.HBM((slots, features), bf16),
             pltpu.HBM((rows, width), bf16),
         ),
-        in_specs=[vmem, hbm, hbm],
+        in_specs=[vmem, vmem, vmem, hbm, hbm],
         out_specs=(hbm, hbm, hbm),
         scratch_shapes=[
             held(features, units),
@@ -264,7 +282,7 @@
         compiler_params=params(),
         cost_estimate=cost(3, 2),
         name="expert",
-    )(landed, in_hbm(up_weight[0]), in_hbm(down_weight[0]))
+    )(landed, in_vmem(first_up), in_vmem(first_down), *weights)
     returned = exchange(back)
 
     down_grad = pl.pallas_call(

time: 87.2 us -> 86 us (0.986)
  Pallas kernels: 27.9 us -> 26.7 us
    pallas_call x1, Pallas kernels: 14.5 us -> 12.7 us  [shards(): pl.pallas_call(functools.partial(expert_kernel, capacity), out_shape=(plt...]
where the time goes in v2:
time: 86 us; the launch traced here: 85.6 us
  blocking collectives  44.7 us (52%)
  Pallas kernels  26.7 us (31%)
  waiting for transfers between devices  10.4 us (12%)
  starting transfers between devices  3.16 us (4%)
    all_to_all x1, blocking collectives, exchange(): lax.all_to_all(cut, axes, split_axis=0, concat_axis=0, tiled=True)  44.7 us
    pallas_call x1, Pallas kernels, shards(): pl.pallas_call(functools.partial(expert_kernel, capacity), out_shape=(plt...  12.7 us
    all_to_all x1, waiting for transfers between devices, exchange(): lax.all_to_all(cut, axes, split_axis=0, concat_axis=0, tiled=True)  10.4 us
    pallas_call x1, Pallas kernels, shards(): pl.pallas_call(down_grad_kernel, out_shape=shape((1, units, features), bf...  10.1 us
    all_to_all x1, starting transfers between devices, exchange(): lax.all_to_all(cut, axes, split_axis=0, concat_axis=0, tiled=True)  3.16 us
    pallas_call x1, Pallas kernels, shards(): pl.pallas_call(functools.partial(dispatch_kernel, capacity), out_shape=(s...  2.49 us
  transfers between devices with their start and end apart: 1, of which 1 were waited for; matrix products, arithmetic and copies ran while one was open for 0% of the time, Pallas kernels for 12%

profile of v2, /device:TPU:1, one launch (start us, length us, event | category | flops | bytes accessed | tf_op | source)
XLA Modules:
  0.0 85.6 jit_solution(11018620619200623135)
XLA Ops:
  0.6 2.5 %dispatch.1 = (bf16[768,1024]{1,0:T(8,128)(2,1)S(1)}, bf16[1024,1024]{1,0:T(8,128)(2,1)S(1)}, bf16[1024,1024]{1,0:T(8,128)(2,1)S(1)}) custom-call(s32[2,128]{1,0:T(2,128)} %bitcast.11, f32[2,128]{1,0:T(2,128)} %bitcast.18, bf16[128,1024]{1,0:T(8,128)(2,1)} %refs_2_.1, bf16[128,1024]{1,0:T(8,128)(2,1)} %refs_3_.1, bf16[1024,4096]{1,0:T(8,128)(2,1)} %bitcast.13, ...), custom_call_target="tpu_custom_call" | custom-call | tf_op jit(solution)/shard_map/dispatch/pallas_call | solution.py:240
  3.1 44.7 %all_to_all.10 = bf16[32,24,1024]{2,1,0:T(8,128)(2,1)S(1)} all-to-all(bf16[32,24,1024]{2,1,0:T(8,128)(2,1)S(1)} %bitcast.10), channel_id=1, replica_groups=mesh['rep'=1,'row'=8,'col'=4] {'row','col'}, dimensions={0} | all-to-all | bytes 3145728 | tf_op jit(solution)/shard_map/all_to_all | solution.py:199
  47.8 0.0 copy-start
  47.8 12.7 %expert.1 = (bf16[384,4096]{1,0:T(8,128)(2,1)}, bf16[384,1024]{1,0:T(8,128)(2,1)}, bf16[768,512]{1,0:T(8,128)(2,1)}) custom-call(bf16[768,1024]{1,0:T(8,128)(2,1)S(1)} %bitcast.9, bf16[1024,1024]{1,0:T(8,128)(2,1)S(1)} %get-tuple-element.9.first_up, bf16[1024,1024]{1,0:T(8,128)(2,1)S(1)} %get-tuple-element.10.first_down, bf16[1024,4096]{1,0:T(8,128)(2,1)} %bitcast.14, ...), custom_call_target="tpu_custom_call" | custom-call | flops 9663676416 | bytes 16777216 | tf_op jit(solution)/shard_map/expert/pallas_call | solution.py:259
  60.5 3.2 %all-to-all-start.1 = ((bf16[32,24,512]{2,1,0:T(8,128)(2,1)}), bf16[32,24,512]{2,1,0:T(8,128)(2,1)S(1)}, u32[]{:S(2)}, u32[]{:S(2)}) async-start(bf16[32,24,512]{2,1,0:T(8,128)(2,1)} %bitcast.17), calls=%async_computation.1 | async-start | bytes 1572864 | tf_op jit(solution)/shard_map/all_to_all | solution.py:199
  63.7 0.0 copy-done
  63.7 0.3 pick_map.1.map_ref
  64.0 10.1 %down_grad.1 = bf16[1,4096,1024]{2,1,0:T(8,128)(2,1)} custom-call(bf16[384,1024]{1,0:T(8,128)(2,1)} %get-tuple-element.11.after_ref.grads_ref, bf16[384,4096]{1,0:T(8,128)(2,1)} %get-tuple-element.13.hidden_ref), custom_call_target="tpu_custom_call" | custom-call | flops 3221225472 | bytes 8388608 | tf_op jit(solution)/shard_map/down_grad/pallas_call | solution.py:288
  74.1 10.4 %all-to-all-done.1 = bf16[32,24,512]{2,1,0:T(8,128)(2,1)S(1)} async-done(((bf16[32,24,512]{2,1,0:T(8,128)(2,1)}), bf16[32,24,512]{2,1,0:T(8,128)(2,1)S(1)}, u32[]{:S(2)}, u32[]{:S(2)}) %all-to-all-start.1) | async-done | bytes 786464 | tf_op jit(solution)/shard_map/all_to_all | solution.py:199
  84.5 1.1 %pick.1 = bf16[128,1024]{1,0:T(8,128)(2,1)} custom-call(bf16[256,768]{1,0:T(8,128)(2,1)S(1)} %pick_map.1.map_ref, bf16[768,512]{1,0:T(8,128)(2,1)S(1)} %bitcast.8), custom_call_target="tpu_custom_call" | custom-call | tf_op jit(solution)/shard_map/pick/pallas_call | solution.py:306
Async XLA Ops:
  47.8 15.9 %copy-start = (s32[128,2]{0,1:T(2,128)S(1)}, s32[128,2]{0,1:T(2,128)}, u32[]{:S(2)}) copy-start(s32[128,2]{0,1:T(2,128)} %param.8) | copy-start | bytes 3076
  60.5 24.0 %all-to-all-start.1 = ((bf16[32,24,512]{2,1,0:T(8,128)(2,1)}), bf16[32,24,512]{2,1,0:T(8,128)(2,1)S(1)}, u32[]{:S(2)}, u32[]{:S(2)}) async-start(bf16[32,24,512]{2,1,0:T(8,128)(2,1)} %bitcast.17), calls=%async_computation.1 | async-start | bytes 1572864 | tf_op jit(solution)/shard_map/all_to_all | solution.py:199

commit v3 on v2

--- a/solution.py
+++ b/solution.py
@@ -53,13 +53,12 @@
 
 
 def dispatch_kernel(capacity, *refs):
-    sources, (up_ref, down_ref, out_ref, up_out, down_out, ids_ref, gates_ref, both_ref, sems) = refs[:4], refs[4:]
+    sources, (up_ref, out_ref, up_out, ids_ref, gates_ref, both_ref, sems) = refs[:4], refs[4:]
     tok_rows = both_ref.shape[0] // 2
     targets = ids_ref, gates_ref, both_ref.at[pl.ds(0, tok_rows)], both_ref.at[pl.ds(tok_rows, tok_rows)]
     ids_copy, gates_copy, tokens_copy, grad_copy = started(zip(sources, targets), sems)
-    first = pl.ds(0, down_out.shape[0])
-    weights = (up_ref.at[:, first], up_out), (down_ref.at[first], down_out)
-    weight_copies = started(weights, sems.at[pl.ds(4, 2)])
+    first_tile = pltpu.make_async_copy(up_ref.at[:, pl.ds(0, up_out.shape[1])], up_out, sems.at[4])
+    first_tile.start()
     rows = out_ref.shape[0]
     ids_copy.wait()
     places = row_places(ids_ref[...], rows // (PAIR * capacity), capacity)
@@ -73,8 +72,7 @@
     tokens_copy.wait()
     grad_copy.wait()
     out_ref[...] = (scale * f32_dot(gather, both_ref[...])).astype(jnp.bfloat16)
-    for copy in weight_copies:
-        copy.wait()
+    first_tile.wait()
 
 
 def paired_rows(number, capacity):
@@ -125,17 +123,17 @@
 
 
 def expert_kernel(
-    capacity, landed_ref, first_up, first_down, up_ref, down_ref, hidden_out, grads_out, back_out, *scratch
+    capacity, landed_ref, first_up, up_ref, down_ref, hidden_out, grads_out, back_out, *scratch
 ):
     up, down, rows, grads, hidden, masked, total, back, weight_sems, hidden_sems, grads_sem, back_sems = scratch
     tiles = unit_tiles(up.shape[1])
 
     def weight_copies(i):
         at = pl.ds(*tiles[i])
-        return [
-            pltpu.make_async_copy(up_ref.at[:, at], up.at[:, at], weight_sems.at[0, i]),
-            pltpu.make_async_copy(down_ref.at[at], down.at[at], weight_sems.at[1, i]),
-        ]
+        copies = [pltpu.make_async_copy(down_ref.at[at], down.at[at], weight_sems.at[1, i])]
+        if i:
+            copies.append(pltpu.make_async_copy(up_ref.at[:, at], up.at[:, at], weight_sems.at[0, i]))
+        return copies
 
     def start_weights(i):
         if i < len(tiles):
@@ -150,18 +148,20 @@
         total[...] = part if i == 0 else total[...] + part
 
     arriving, leaving = {}, []
+    start_weights(0)
+    take_apart(landed_ref, capacity, rows, grads)
     for i in range(1, AHEAD):
         start_weights(i)
-    take_apart(landed_ref, capacity, rows, grads)
     leaving.append(pltpu.make_async_copy(grads, grads_out, grads_sem.at[0]))
     leaving[-1].start()
     for i, (start, size) in enumerate(tiles):
         here = slice(start, start + size)
         start_weights(i + AHEAD)
-        for copy in arriving.get(i, ()):
+        for copy in arriving[i][1:]:
             copy.wait()
         preact = f32_dot(rows[...], up[:, here] if i else first_up[...])
-        hidden_grad = f32_dot(grads[...], down[here, :] if i else first_down[...], ((1,), (1,)))
+        arriving[i][0].wait()
+        hidden_grad = f32_dot(grads[...], down[here, :], ((1,), (1,)))
         if i:
             add_row_grad(i - 1)
         hidden[:, here] = jnp.maximum(preact, 0.0).astype(jnp.bfloat16)
@@ -237,23 +237,22 @@
 
     size = tiles[0][1]
     weights = in_hbm(up_weight[0]), in_hbm(down_weight[0])
-    sent, first_up, first_down = pl.pallas_call(
+    sent, first_up = pl.pallas_call(
         functools.partial(dispatch_kernel, capacity),
         out_shape=(
             shape((rows, features), bf16),
             pltpu.VMEM((features, size), bf16),
-            pltpu.VMEM((size, features), bf16),
         ),
-        in_specs=[hbm, hbm, hbm, hbm, hbm, hbm],
+        in_specs=[hbm, hbm, hbm, hbm, hbm],
         scratch_shapes=[
             held(top_count, tok_rows, jnp.int32),
             held(top_count, tok_rows, f32),
             held(2 * tok_rows, features),
-            dma((6,)),
+            dma((5,)),
         ],
         compiler_params=params(),
         name="dispatch",
-    )(*[in_hbm(array) for array in (ids, gates.T, tokens, out_grad)], *weights)
+    )(*[in_hbm(array) for array in (ids, gates.T, tokens, out_grad)], weights[0])
     landed = exchange(sent)
 
     hidden, grads, back = pl.pallas_call(
@@ -263,7 +262,7 @@
             pltpu.HBM((slots, features), bf16),
             pltpu.HBM((rows, width), bf16),
         ),
-        in_specs=[vmem, vmem, vmem, hbm, hbm],
+        in_specs=[vmem, vmem, hbm, hbm],
         out_specs=(hbm, hbm, hbm),
         scratch_shapes=[
             held(features, units),
@@ -282,7 +281,7 @@
         compiler_params=params(),
         cost_estimate=cost(3, 2),
         name="expert",
-    )(landed, in_vmem(first_up), in_vmem(first_down), *weights)
+    )(landed, in_vmem(first_up), *weights)
     returned = exchange(back)
 
     down_grad = pl.pallas_call(

time: 86 us -> 87.1 us (1.013)
  Pallas kernels: 26.7 us -> 27.7 us
    pallas_call x1, Pallas kernels: 12.7 us -> 14.3 us  [shards(): pl.pallas_call(functools.partial(expert_kernel, capacity), out_shape=(plt...]
where the time goes in v3:
time: 87.1 us; the launch traced here: 86.6 us
  blocking collectives  44.7 us (51%)
  Pallas kernels  27.7 us (32%)
  waiting for transfers between devices  10.4 us (12%)
  starting transfers between devices  3.16 us (4%)
    all_to_all x1, blocking collectives, exchange(): lax.all_to_all(cut, axes, split_axis=0, concat_axis=0, tiled=True)  44.7 us
    pallas_call x1, Pallas kernels, shards(): pl.pallas_call(functools.partial(expert_kernel, capacity), out_shape=(plt...  14.3 us
    all_to_all x1, waiting for transfers between devices, exchange(): lax.all_to_all(cut, axes, split_axis=0, concat_axis=0, tiled=True)  10.4 us
    pallas_call x1, Pallas kernels, shards(): pl.pallas_call(down_grad_kernel, out_shape=shape((1, units, features), bf...  10.1 us
    all_to_all x1, starting transfers between devices, exchange(): lax.all_to_all(cut, axes, split_axis=0, concat_axis=0, tiled=True)  3.16 us
    pallas_call x1, Pallas kernels, shards(): pl.pallas_call(functools.partial(dispatch_kernel, capacity), out_shape=(s...  1.9 us
  transfers between devices with their start and end apart: 1, of which 1 were waited for; matrix products, arithmetic and copies ran while one was open for 0% of the time, Pallas kernels for 12%

profile of v3, /device:TPU:1, one launch (start us, length us, event | category | flops | bytes accessed | tf_op | source)
XLA Modules:
  0.0 86.6 jit_solution(179619866275491733)
XLA Ops:
  0.6 1.9 %dispatch.1 = (bf16[768,1024]{1,0:T(8,128)(2,1)S(1)}, bf16[1024,1024]{1,0:T(8,128)(2,1)S(1)}) custom-call(s32[2,128]{1,0:T(2,128)} %bitcast.11, f32[2,128]{1,0:T(2,128)} %bitcast.16, bf16[128,1024]{1,0:T(8,128)(2,1)} %refs_2_.1, bf16[128,1024]{1,0:T(8,128)(2,1)} %refs_3_.1, bf16[1024,4096]{1,0:T(8,128)(2,1)} %bitcast.13), custom_call_target="tpu_custom_call" | custom-call | tf_op jit(solution)/shard_map/dispatch/pallas_call | solution.py:240
  2.5 44.7 %all_to_all.10 = bf16[32,24,1024]{2,1,0:T(8,128)(2,1)S(1)} all-to-all(bf16[32,24,1024]{2,1,0:T(8,128)(2,1)S(1)} %bitcast.10), channel_id=1, replica_groups=mesh['rep'=1,'row'=8,'col'=4] {'row','col'}, dimensions={0} | all-to-all | bytes 3145728 | tf_op jit(solution)/shard_map/all_to_all | solution.py:199
  47.2 0.0 copy-start
  47.2 14.3 %expert.1 = (bf16[384,4096]{1,0:T(8,128)(2,1)}, bf16[384,1024]{1,0:T(8,128)(2,1)}, bf16[768,512]{1,0:T(8,128)(2,1)}) custom-call(bf16[768,1024]{1,0:T(8,128)(2,1)S(1)} %bitcast.9, bf16[1024,1024]{1,0:T(8,128)(2,1)S(1)} %get-tuple-element.8.first_up, bf16[1024,4096]{1,0:T(8,128)(2,1)} %bitcast.14, bf16[4096,1024]{1,0:T(8,128)(2,1)} %bitcast.17), custom_call_target="tpu_custom_call" | custom-call | flops 9663676416 | bytes 16777216 | tf_op jit(solution)/shard_map/expert/pallas_call | solution.py:258
  61.6 3.2 %all-to-all-start.1 = ((bf16[32,24,512]{2,1,0:T(8,128)(2,1)}), bf16[32,24,512]{2,1,0:T(8,128)(2,1)S(1)}, u32[]{:S(2)}, u32[]{:S(2)}) async-start(bf16[32,24,512]{2,1,0:T(8,128)(2,1)} %bitcast.15), calls=%async_computation.1 | async-start | bytes 1572864 | tf_op jit(solution)/shard_map/all_to_all | solution.py:199
  64.7 0.0 copy-done
  64.7 0.3 pick_map.1.map_ref
  65.1 10.1 %down_grad.1 = bf16[1,4096,1024]{2,1,0:T(8,128)(2,1)} custom-call(bf16[384,1024]{1,0:T(8,128)(2,1)} %get-tuple-element.9.after_ref.grads_ref, bf16[384,4096]{1,0:T(8,128)(2,1)} %get-tuple-element.11.hidden_ref), custom_call_target="tpu_custom_call" | custom-call | flops 3221225472 | bytes 8388608 | tf_op jit(solution)/shard_map/down_grad/pallas_call | solution.py:287
  75.2 10.4 %all-to-all-done.1 = bf16[32,24,512]{2,1,0:T(8,128)(2,1)S(1)} async-done(((bf16[32,24,512]{2,1,0:T(8,128)(2,1)}), bf16[32,24,512]{2,1,0:T(8,128)(2,1)S(1)}, u32[]{:S(2)}, u32[]{:S(2)}) %all-to-all-start.1) | async-done | bytes 786464 | tf_op jit(solution)/shard_map/all_to_all | solution.py:199
  85.6 1.1 %pick.1 = bf16[128,1024]{1,0:T(8,128)(2,1)} custom-call(bf16[256,768]{1,0:T(8,128)(2,1)S(1)} %pick_map.1.map_ref, bf16[768,512]{1,0:T(8,128)(2,1)S(1)} %bitcast.8), custom_call_target="tpu_custom_call" | custom-call | tf_op jit(solution)/shard_map/pick/pallas_call | solution.py:305
Async XLA Ops:
  47.2 17.5 %copy-start = (s32[128,2]{0,1:T(2,128)S(1)}, s32[128,2]{0,1:T(2,128)}, u32[]{:S(2)}) copy-start(s32[128,2]{0,1:T(2,128)} %param.8) | copy-start | bytes 3076
  61.6 24.0 %all-to-all-start.1 = ((bf16[32,24,512]{2,1,0:T(8,128)(2,1)}), bf16[32,24,512]{2,1,0:T(8,128)(2,1)S(1)}, u32[]{:S(2)}, u32[]{:S(2)}) async-start(bf16[32,24,512]{2,1,0:T(8,128)(2,1)} %bitcast.15), calls=%async_computation.1 | async-start | bytes 1572864 | tf_op jit(solution)/shard_map/all_to_all | solution.py:199

commit v4 on v2

--- a/solution.py
+++ b/solution.py
@@ -11,6 +11,7 @@
 PAIR = 2
 TILE = 1024
 AHEAD = 2
+PIECES = 4
 NOWHERE = -(1 << 20)
 
 
@@ -131,11 +132,15 @@
     tiles = unit_tiles(up.shape[1])
 
     def weight_copies(i):
-        at = pl.ds(*tiles[i])
-        return [
-            pltpu.make_async_copy(up_ref.at[:, at], up.at[:, at], weight_sems.at[0, i]),
-            pltpu.make_async_copy(down_ref.at[at], down.at[at], weight_sems.at[1, i]),
-        ]
+        start, size = tiles[i]
+        copies = []
+        for n in range(PIECES):
+            part = pl.ds(n * (up.shape[0] // PIECES), up.shape[0] // PIECES), pl.ds(start, size)
+            copies.append(pltpu.make_async_copy(up_ref.at[part], up.at[part], weight_sems.at[0, i, n]))
+        for n in range(PIECES):
+            part = pl.ds(start + n * (size // PIECES), size // PIECES)
+            copies.append(pltpu.make_async_copy(down_ref.at[part], down.at[part], weight_sems.at[1, i, n]))
+        return copies
 
     def start_weights(i):
         if i < len(tiles):
@@ -274,7 +279,7 @@
             pltpu.VMEM((2, slots, tiles[0][1]), bf16),
             held(slots, features, f32),
             held(rows, width),
-            dma((2, len(tiles))),
+            dma((2, len(tiles), PIECES)),
             dma((len(tiles),)),
             dma((1,)),
             dma((peers // group_size(peers, capacity),)),

time: 86 us -> 87.3 us (1.015)
  Pallas kernels: 26.7 us -> 28 us
    pallas_call x1, Pallas kernels: 12.7 us -> 14 us  [shards(): pl.pallas_call(functools.partial(expert_kernel, capacity), out_shape=(plt...]
where the time goes in v4:
time: 87.3 us; the launch traced here: 86.9 us
  blocking collectives  44.7 us (51%)
  Pallas kernels  28 us (32%)
  waiting for transfers between devices  10.4 us (12%)
  starting transfers between devices  3.15 us (4%)
    all_to_all x1, blocking collectives, exchange(): lax.all_to_all(cut, axes, split_axis=0, concat_axis=0, tiled=True)  44.7 us
    pallas_call x1, Pallas kernels, shards(): pl.pallas_call(functools.partial(expert_kernel, capacity), out_shape=(plt...  14 us
    all_to_all x1, waiting for transfers between devices, exchange(): lax.all_to_all(cut, axes, split_axis=0, concat_axis=0, tiled=True)  10.4 us
    pallas_call x1, Pallas kernels, shards(): pl.pallas_call(down_grad_kernel, out_shape=shape((1, units, features), bf...  10.1 us
    all_to_all x1, starting transfers between devices, exchange(): lax.all_to_all(cut, axes, split_axis=0, concat_axis=0, tiled=True)  3.15 us
    pallas_call x1, Pallas kernels, shards(): pl.pallas_call(functools.partial(dispatch_kernel, capacity), out_shape=(s...  2.49 us
  transfers between devices with their start and end apart: 1, of which 1 were waited for; matrix products, arithmetic and copies ran while one was open for 0% of the time, Pallas kernels for 12%

profile of v4, /device:TPU:1, one launch (start us, length us, event | category | flops | bytes accessed | tf_op | source)
XLA Modules:
  0.0 86.9 jit_solution(8690261059592279287)
XLA Ops:
  0.6 2.5 %dispatch.1 = (bf16[768,1024]{1,0:T(8,128)(2,1)S(1)}, bf16[1024,1024]{1,0:T(8,128)(2,1)S(1)}, bf16[1024,1024]{1,0:T(8,128)(2,1)S(1)}) custom-call(s32[2,128]{1,0:T(2,128)} %bitcast.11, f32[2,128]{1,0:T(2,128)} %bitcast.18, bf16[128,1024]{1,0:T(8,128)(2,1)} %refs_2_.1, bf16[128,1024]{1,0:T(8,128)(2,1)} %refs_3_.1, bf16[1024,4096]{1,0:T(8,128)(2,1)} %bitcast.13, ...), custom_call_target="tpu_custom_call" | custom-call | tf_op jit(solution)/shard_map/dispatch/pallas_call | solution.py:245
  3.1 44.7 %all_to_all.10 = bf16[32,24,1024]{2,1,0:T(8,128)(2,1)S(1)} all-to-all(bf16[32,24,1024]{2,1,0:T(8,128)(2,1)S(1)} %bitcast.10), channel_id=1, replica_groups=mesh['rep'=1,'row'=8,'col'=4] {'row','col'}, dimensions={0} | all-to-all | bytes 3145728 | tf_op jit(solution)/shard_map/all_to_all | solution.py:204
  47.8 0.0 copy-start
  47.8 14.0 %expert.1 = (bf16[384,4096]{1,0:T(8,128)(2,1)}, bf16[384,1024]{1,0:T(8,128)(2,1)}, bf16[768,512]{1,0:T(8,128)(2,1)}) custom-call(bf16[768,1024]{1,0:T(8,128)(2,1)S(1)} %bitcast.9, bf16[1024,1024]{1,0:T(8,128)(2,1)S(1)} %get-tuple-element.9.first_up, bf16[1024,1024]{1,0:T(8,128)(2,1)S(1)} %get-tuple-element.10.first_down, bf16[1024,4096]{1,0:T(8,128)(2,1)} %bitcast.14, ...), custom_call_target="tpu_custom_call" | custom-call | flops 9663676416 | bytes 16777216 | tf_op jit(solution)/shard_map/expert/pallas_call | solution.py:264
  61.9 3.2 %all-to-all-start.1 = ((bf16[32,24,512]{2,1,0:T(8,128)(2,1)}), bf16[32,24,512]{2,1,0:T(8,128)(2,1)S(1)}, u32[]{:S(2)}, u32[]{:S(2)}) async-start(bf16[32,24,512]{2,1,0:T(8,128)(2,1)} %bitcast.17), calls=%async_computation.1 | async-start | bytes 1572864 | tf_op jit(solution)/shard_map/all_to_all | solution.py:204
  65.0 0.0 copy-done
  65.0 0.3 pick_map.1.map_ref
  65.3 10.1 %down_grad.1 = bf16[1,4096,1024]{2,1,0:T(8,128)(2,1)} custom-call(bf16[384,1024]{1,0:T(8,128)(2,1)} %get-tuple-element.11.after_ref.grads_ref, bf16[384,4096]{1,0:T(8,128)(2,1)} %get-tuple-element.13.hidden_ref), custom_call_target="tpu_custom_call" | custom-call | flops 3221225472 | bytes 8388608 | tf_op jit(solution)/shard_map/down_grad/pallas_call | solution.py:293
  75.4 10.4 %all-to-all-done.1 = bf16[32,24,512]{2,1,0:T(8,128)(2,1)S(1)} async-done(((bf16[32,24,512]{2,1,0:T(8,128)(2,1)}), bf16[32,24,512]{2,1,0:T(8,128)(2,1)S(1)}, u32[]{:S(2)}, u32[]{:S(2)}) %all-to-all-start.1) | async-done | bytes 786464 | tf_op jit(solution)/shard_map/all_to_all | solution.py:204
  85.8 1.1 %pick.1 = bf16[128,1024]{1,0:T(8,128)(2,1)} custom-call(bf16[256,768]{1,0:T(8,128)(2,1)S(1)} %pick_map.1.map_ref, bf16[768,512]{1,0:T(8,128)(2,1)S(1)} %bitcast.8), custom_call_target="tpu_custom_call" | custom-call | tf_op jit(solution)/shard_map/pick/pallas_call | solution.py:311
Async XLA Ops:
  47.8 17.2 %copy-start = (s32[128,2]{0,1:T(2,128)S(1)}, s32[128,2]{0,1:T(2,128)}, u32[]{:S(2)}) copy-start(s32[128,2]{0,1:T(2,128)} %param.8) | copy-start | bytes 3076
  61.9 24.0 %all-to-all-start.1 = ((bf16[32,24,512]{2,1,0:T(8,128)(2,1)}), bf16[32,24,512]{2,1,0:T(8,128)(2,1)S(1)}, u32[]{:S(2)}, u32[]{:S(2)}) async-start(bf16[32,24,512]{2,1,0:T(8,128)(2,1)} %bitcast.17), calls=%async_computation.1 | async-start | bytes 1572864 | tf_op jit(solution)/shard_map/all_to_all | solution.py:204

commit v5 on v2

--- a/solution.py
+++ b/solution.py
@@ -10,7 +10,6 @@
 VMEM_LIMIT = 44 * 1024 * 1024
 PAIR = 2
 TILE = 1024
-AHEAD = 2
 NOWHERE = -(1 << 20)
 
 
@@ -150,16 +149,16 @@
         total[...] = part if i == 0 else total[...] + part
 
     arriving, leaving = {}, []
-    for i in range(1, AHEAD):
-        start_weights(i)
+    start_weights(1)
     take_apart(landed_ref, capacity, rows, grads)
     leaving.append(pltpu.make_async_copy(grads, grads_out, grads_sem.at[0]))
     leaving[-1].start()
     for i, (start, size) in enumerate(tiles):
         here = slice(start, start + size)
-        start_weights(i + AHEAD)
         for copy in arriving.get(i, ()):
             copy.wait()
+        if i:
+            start_weights(i + 1)
         preact = f32_dot(rows[...], up[:, here] if i else first_up[...])
         hidden_grad = f32_dot(grads[...], down[here, :] if i else first_down[...], ((1,), (1,)))
         if i:

time: 86 us -> 87.2 us (1.014)
  Pallas kernels: 26.7 us -> 27.9 us
    pallas_call x1, Pallas kernels: 12.7 us -> 14 us  [shards(): pl.pallas_call(functools.partial(expert_kernel, capacity), out_shape=(plt...]
where the time goes in v5:
time: 87.2 us; the launch traced here: 86.8 us
  blocking collectives  44.7 us (51%)
  Pallas kernels  27.9 us (32%)
  waiting for transfers between devices  10.4 us (12%)
  starting transfers between devices  3.16 us (4%)
    all_to_all x1, blocking collectives, exchange(): lax.all_to_all(cut, axes, split_axis=0, concat_axis=0, tiled=True)  44.7 us
    pallas_call x1, Pallas kernels, shards(): pl.pallas_call(functools.partial(expert_kernel, capacity), out_shape=(plt...  14 us
    all_to_all x1, waiting for transfers between devices, exchange(): lax.all_to_all(cut, axes, split_axis=0, concat_axis=0, tiled=True)  10.4 us
    pallas_call x1, Pallas kernels, shards(): pl.pallas_call(down_grad_kernel, out_shape=shape((1, units, features), bf...  10.1 us
    all_to_all x1, starting transfers between devices, exchange(): lax.all_to_all(cut, axes, split_axis=0, concat_axis=0, tiled=True)  3.16 us
    pallas_call x1, Pallas kernels, shards(): pl.pallas_call(functools.partial(dispatch_kernel, capacity), out_shape=(s...  2.49 us
  transfers between devices with their start and end apart: 1, of which 1 were waited for; matrix products, arithmetic and copies ran while one was open for 0% of the time, Pallas kernels for 12%

profile of v5, /device:TPU:1, one launch (start us, length us, event | category | flops | bytes accessed | tf_op | source)
XLA Modules:
  0.0 86.8 jit_solution(1044398702211000719)
XLA Ops:
  0.6 2.5 %dispatch.1 = (bf16[768,1024]{1,0:T(8,128)(2,1)S(1)}, bf16[1024,1024]{1,0:T(8,128)(2,1)S(1)}, bf16[1024,1024]{1,0:T(8,128)(2,1)S(1)}) custom-call(s32[2,128]{1,0:T(2,128)} %bitcast.11, f32[2,128]{1,0:T(2,128)} %bitcast.18, bf16[128,1024]{1,0:T(8,128)(2,1)} %refs_2_.1, bf16[128,1024]{1,0:T(8,128)(2,1)} %refs_3_.1, bf16[1024,4096]{1,0:T(8,128)(2,1)} %bitcast.13, ...), custom_call_target="tpu_custom_call" | custom-call | tf_op jit(solution)/shard_map/dispatch/pallas_call | solution.py:239
  3.1 44.7 %all_to_all.10 = bf16[32,24,1024]{2,1,0:T(8,128)(2,1)S(1)} all-to-all(bf16[32,24,1024]{2,1,0:T(8,128)(2,1)S(1)} %bitcast.10), channel_id=1, replica_groups=mesh['rep'=1,'row'=8,'col'=4] {'row','col'}, dimensions={0} | all-to-all | bytes 3145728 | tf_op jit(solution)/shard_map/all_to_all | solution.py:198
  47.8 0.0 copy-start
  47.8 14.0 %expert.1 = (bf16[384,4096]{1,0:T(8,128)(2,1)}, bf16[384,1024]{1,0:T(8,128)(2,1)}, bf16[768,512]{1,0:T(8,128)(2,1)}) custom-call(bf16[768,1024]{1,0:T(8,128)(2,1)S(1)} %bitcast.9, bf16[1024,1024]{1,0:T(8,128)(2,1)S(1)} %get-tuple-element.9.first_up, bf16[1024,1024]{1,0:T(8,128)(2,1)S(1)} %get-tuple-element.10.first_down, bf16[1024,4096]{1,0:T(8,128)(2,1)} %bitcast.14, ...), custom_call_target="tpu_custom_call" | custom-call | flops 9663676416 | bytes 16777216 | tf_op jit(solution)/shard_map/expert/pallas_call | solution.py:258
  61.8 3.2 %all-to-all-start.1 = ((bf16[32,24,512]{2,1,0:T(8,128)(2,1)}), bf16[32,24,512]{2,1,0:T(8,128)(2,1)S(1)}, u32[]{:S(2)}, u32[]{:S(2)}) async-start(bf16[32,24,512]{2,1,0:T(8,128)(2,1)} %bitcast.17), calls=%async_computation.1 | async-start | bytes 1572864 | tf_op jit(solution)/shard_map/all_to_all | solution.py:198
  64.9 0.0 copy-done
  64.9 0.3 pick_map.1.map_ref
  65.3 10.1 %down_grad.1 = bf16[1,4096,1024]{2,1,0:T(8,128)(2,1)} custom-call(bf16[384,1024]{1,0:T(8,128)(2,1)} %get-tuple-element.11.after_ref.grads_ref, bf16[384,4096]{1,0:T(8,128)(2,1)} %get-tuple-element.13.hidden_ref), custom_call_target="tpu_custom_call" | custom-call | flops 3221225472 | bytes 8388608 | tf_op jit(solution)/shard_map/down_grad/pallas_call | solution.py:287
  75.4 10.4 %all-to-all-done.1 = bf16[32,24,512]{2,1,0:T(8,128)(2,1)S(1)} async-done(((bf16[32,24,512]{2,1,0:T(8,128)(2,1)}), bf16[32,24,512]{2,1,0:T(8,128)(2,1)S(1)}, u32[]{:S(2)}, u32[]{:S(2)}) %all-to-all-start.1) | async-done | bytes 786464 | tf_op jit(solution)/shard_map/all_to_all | solution.py:198
  85.8 1.1 %pick.1 = bf16[128,1024]{1,0:T(8,128)(2,1)} custom-call(bf16[256,768]{1,0:T(8,128)(2,1)S(1)} %pick_map.1.map_ref, bf16[768,512]{1,0:T(8,128)(2,1)S(1)} %bitcast.8), custom_call_target="tpu_custom_call" | custom-call | tf_op jit(solution)/shard_map/pick/pallas_call | solution.py:305
Async XLA Ops:
  47.8 17.1 %copy-start = (s32[128,2]{0,1:T(2,128)S(1)}, s32[128,2]{0,1:T(2,128)}, u32[]{:S(2)}) copy-start(s32[128,2]{0,1:T(2,128)} %param.8) | copy-start | bytes 3076
  61.8 24.0 %all-to-all-start.1 = ((bf16[32,24,512]{2,1,0:T(8,128)(2,1)}), bf16[32,24,512]{2,1,0:T(8,128)(2,1)S(1)}, u32[]{:S(2)}, u32[]{:S(2)}) async-start(bf16[32,24,512]{2,1,0:T(8,128)(2,1)} %bitcast.17), calls=%async_computation.1 | async-start | bytes 1572864 | tf_op jit(solution)/shard_map/all_to_all | solution.py:198

commit v6 on v2

--- a/solution.py
+++ b/solution.py
@@ -154,7 +154,6 @@
         start_weights(i)
     take_apart(landed_ref, capacity, rows, grads)
     leaving.append(pltpu.make_async_copy(grads, grads_out, grads_sem.at[0]))
-    leaving[-1].start()
     for i, (start, size) in enumerate(tiles):
         here = slice(start, start + size)
         start_weights(i + AHEAD)
@@ -167,7 +166,8 @@
         hidden[:, here] = jnp.maximum(preact, 0.0).astype(jnp.bfloat16)
         masked[i % 2, :, :size] = jnp.where(preact > 0, hidden_grad, 0.0).astype(jnp.bfloat16)
         leaving.append(pltpu.make_async_copy(hidden.at[:, here], hidden_out.at[:, here], hidden_sems.at[i]))
-        leaving[-1].start()
+    for copy in leaving:
+        copy.start()
     add_row_grad(len(tiles) - 1)
     for copy in leaving + fold_rows(total, capacity, back, back_out, back_sems):
         copy.wait()

time: 86 us -> 85.7 us (level)
  no operation moved by 1% of the time
where the time goes in v6:
time: 85.7 us; the launch traced here: 85.3 us
  blocking collectives  44.7 us (52%)
  Pallas kernels  26.4 us (31%)
  waiting for transfers between devices  10.4 us (12%)
  starting transfers between devices  3.16 us (4%)
    all_to_all x1, blocking collectives, exchange(): lax.all_to_all(cut, axes, split_axis=0, concat_axis=0, tiled=True)  44.7 us
    pallas_call x1, Pallas kernels, shards(): pl.pallas_call(functools.partial(expert_kernel, capacity), out_shape=(plt...  12.4 us
    all_to_all x1, waiting for transfers between devices, exchange(): lax.all_to_all(cut, axes, split_axis=0, concat_axis=0, tiled=True)  10.4 us
    pallas_call x1, Pallas kernels, shards(): pl.pallas_call(down_grad_kernel, out_shape=shape((1, units, features), bf...  10.1 us
    all_to_all x1, starting transfers between devices, exchange(): lax.all_to_all(cut, axes, split_axis=0, concat_axis=0, tiled=True)  3.16 us
    pallas_call x1, Pallas kernels, shards(): pl.pallas_call(functools.partial(dispatch_kernel, capacity), out_shape=(s...  2.49 us
  transfers between devices with their start and end apart: 1, of which 1 were waited for; matrix products, arithmetic and copies ran while one was open for 0% of the time, Pallas kernels for 12%

profile of v6, /device:TPU:1, one launch (start us, length us, event | category | flops | bytes accessed | tf_op | source)
XLA Modules:
  0.0 85.3 jit_solution(4140509395079984400)
XLA Ops:
  0.6 2.5 %dispatch.1 = (bf16[768,1024]{1,0:T(8,128)(2,1)S(1)}, bf16[1024,1024]{1,0:T(8,128)(2,1)S(1)}, bf16[1024,1024]{1,0:T(8,128)(2,1)S(1)}) custom-call(s32[2,128]{1,0:T(2,128)} %bitcast.11, f32[2,128]{1,0:T(2,128)} %bitcast.18, bf16[128,1024]{1,0:T(8,128)(2,1)} %refs_2_.1, bf16[128,1024]{1,0:T(8,128)(2,1)} %refs_3_.1, bf16[1024,4096]{1,0:T(8,128)(2,1)} %bitcast.13, ...), custom_call_target="tpu_custom_call" | custom-call | tf_op jit(solution)/shard_map/dispatch/pallas_call | solution.py:240
  3.1 44.7 %all_to_all.10 = bf16[32,24,1024]{2,1,0:T(8,128)(2,1)S(1)} all-to-all(bf16[32,24,1024]{2,1,0:T(8,128)(2,1)S(1)} %bitcast.10), channel_id=1, replica_groups=mesh['rep'=1,'row'=8,'col'=4] {'row','col'}, dimensions={0} | all-to-all | bytes 3145728 | tf_op jit(solution)/shard_map/all_to_all | solution.py:199
  47.8 0.0 copy-start
  47.8 12.4 %expert.1 = (bf16[384,4096]{1,0:T(8,128)(2,1)}, bf16[384,1024]{1,0:T(8,128)(2,1)}, bf16[768,512]{1,0:T(8,128)(2,1)}) custom-call(bf16[768,1024]{1,0:T(8,128)(2,1)S(1)} %bitcast.9, bf16[1024,1024]{1,0:T(8,128)(2,1)S(1)} %get-tuple-element.9.first_up, bf16[1024,1024]{1,0:T(8,128)(2,1)S(1)} %get-tuple-element.10.first_down, bf16[1024,4096]{1,0:T(8,128)(2,1)} %bitcast.14, ...), custom_call_target="tpu_custom_call" | custom-call | flops 9663676416 | bytes 16777216 | tf_op jit(solution)/shard_map/expert/pallas_call | solution.py:259
  60.2 3.2 %all-to-all-start.1 = ((bf16[32,24,512]{2,1,0:T(8,128)(2,1)}), bf16[32,24,512]{2,1,0:T(8,128)(2,1)S(1)}, u32[]{:S(2)}, u32[]{:S(2)}) async-start(bf16[32,24,512]{2,1,0:T(8,128)(2,1)} %bitcast.17), calls=%async_computation.1 | async-start | bytes 1572864 | tf_op jit(solution)/shard_map/all_to_all | solution.py:199
  63.4 0.0 copy-done
  63.4 0.3 pick_map.1.map_ref
  63.7 10.1 %down_grad.1 = bf16[1,4096,1024]{2,1,0:T(8,128)(2,1)} custom-call(bf16[384,1024]{1,0:T(8,128)(2,1)} %get-tuple-element.11.after_ref.grads_ref, bf16[384,4096]{1,0:T(8,128)(2,1)} %get-tuple-element.13.hidden_ref), custom_call_target="tpu_custom_call" | custom-call | flops 3221225472 | bytes 8388608 | tf_op jit(solution)/shard_map/down_grad/pallas_call | solution.py:288
  73.8 10.4 %all-to-all-done.1 = bf16[32,24,512]{2,1,0:T(8,128)(2,1)S(1)} async-done(((bf16[32,24,512]{2,1,0:T(8,128)(2,1)}), bf16[32,24,512]{2,1,0:T(8,128)(2,1)S(1)}, u32[]{:S(2)}, u32[]{:S(2)}) %all-to-all-start.1) | async-done | bytes 786464 | tf_op jit(solution)/shard_map/all_to_all | solution.py:199
  84.2 1.1 %pick.1 = bf16[128,1024]{1,0:T(8,128)(2,1)} custom-call(bf16[256,768]{1,0:T(8,128)(2,1)S(1)} %pick_map.1.map_ref, bf16[768,512]{1,0:T(8,128)(2,1)S(1)} %bitcast.8), custom_call_target="tpu_custom_call" | custom-call | tf_op jit(solution)/shard_map/pick/pallas_call | solution.py:306
Async XLA Ops:
  47.8 15.6 %copy-start = (s32[128,2]{0,1:T(2,128)S(1)}, s32[128,2]{0,1:T(2,128)}, u32[]{:S(2)}) copy-start(s32[128,2]{0,1:T(2,128)} %param.8) | copy-start | bytes 3076
  60.2 24.0 %all-to-all-start.1 = ((bf16[32,24,512]{2,1,0:T(8,128)(2,1)}), bf16[32,24,512]{2,1,0:T(8,128)(2,1)S(1)}, u32[]{:S(2)}, u32[]{:S(2)}) async-start(bf16[32,24,512]{2,1,0:T(8,128)(2,1)} %bitcast.17), calls=%async_computation.1 | async-start | bytes 1572864 | tf_op jit(solution)/shard_map/all_to_all | solution.py:199
